TPU v7x, 512 devices: a whole 4x4x16 slice. The times are simulated.
512 devices in a mesh: band: 128 (over y, z, core), edge: 4 (over x).
Axes of the slice: x: 4, y: 4, z: 16, core: 2. Of those that a mesh axis runs over, the one named last changes fastest.
Arguments:
- grid_lat: bfloat16 [131072, 512], P('band'), may hold values from -6 to 6
- edge_lat: bfloat16 [65536, 512], P(('band', 'edge')), may hold values from -24 to 24
- send_local: int32 [65536], P(('band', 'edge')), may hold values from 0 to 1023
- dest_band: int32 [65536, 1], P(('band', 'edge')), may hold values from 0 to 127; in each aligned block of 128 rows (0 to 127, 128 to 255, ...) at most 2 rows name the same one
- receiver_in_band: int32 [65536], P(('band', 'edge')), may hold values from 0 to 255
- mesh_lat: bfloat16 [32768, 512], P('band'), may hold values from -6 to 6
- w_edge_in: bfloat16 [512, 512], replicated, may hold values from -0.25 to 0.25
- w_edge_out: bfloat16 [512, 512], replicated, may hold values from -0.25 to 0.25
- w_node_in: bfloat16 [1024, 512], P(None, 'edge'), may hold values from -0.1875 to 0.1875
- w_node_out: bfloat16 [512, 512], P('edge'), may hold values from -0.25 to 0.25
- norm_gain: float32 [512], replicated, may hold values from 0.25 to 1.75
- cotangent: bfloat16 [32768, 512], P('band'), may hold values from -6 to 6
Outputs:
- new_mesh: bfloat16 [32768, 512], P('band')
- grad_edge_in: float32 [512, 512], P(('band', 'edge'))
- grad_edge_out: float32 [512, 512], P(('band', 'edge'))
Inputs may be any that keep to these rules, and one draw needn't show every extreme that they name: Among the 128 edges of one device at most 2 have any one band in dest_band; in some devices one band has exactly 2.
All inputs are finite; a program needn't handle non-finite values.
Results may differ from a plain program's by a relative error of at most 0.02.
Values may be sent and summed in bfloat16 or wider, within the bound.
A program may use at most 64 MiB of HBM per device.

v0:
```python
import jax
import jax.numpy as jnp
from jax import lax
from jax.sharding import PartitionSpec as P


def swish_grad(value):
    sig = jax.nn.sigmoid(value)
    return sig * (1.0 + value * (1.0 - sig))


def edge_forward(x_in, w_edge_in, w_edge_out):
    z_edge = jnp.dot(x_in, w_edge_in, preferred_element_type=jnp.float32)
    h_edge = jax.nn.silu(z_edge).astype(jnp.bfloat16)
    message = lax.dot_general(
        h_edge, w_edge_out, (((1,), (1,)), ((), ())), preferred_element_type=jnp.float32
    )
    return (z_edge, h_edge, message.astype(jnp.bfloat16))


def edge_backward(x_in, z_edge, h_edge, message_gradient, w_edge_out):
    dh_edge = jnp.dot(message_gradient, w_edge_out, preferred_element_type=jnp.float32)
    dz_edge = (dh_edge * swish_grad(z_edge)).astype(jnp.bfloat16)
    grad_in = lax.dot_general(
        x_in, dz_edge, (((0,), (0,)), ((), ())), preferred_element_type=jnp.float32
    )
    grad_out = lax.dot_general(
        message_gradient, h_edge, (((0,), (0,)), ((), ())), preferred_element_type=jnp.float32
    )
    return (grad_in, grad_out)


def norm_rows(y_out, base, gain, upstream_raw):
    mean_y = jnp.mean(y_out, axis=1, keepdims=True)
    centred = y_out - mean_y
    inv_std = lax.rsqrt(jnp.mean(centred * centred, axis=1, keepdims=True) + 1e-05)
    normed = centred * inv_std
    new_rows = (base.astype(jnp.float32) + normed * gain).astype(jnp.bfloat16)
    upstream = upstream_raw.astype(jnp.float32) * gain
    d_y = (
        upstream
        - jnp.mean(upstream, axis=1, keepdims=True)
        - normed * jnp.mean(upstream * normed, axis=1, keepdims=True)
    ) * inv_std
    return (new_rows, d_y.astype(jnp.bfloat16))


def node_backward(d_y, z_node, w_in, w_out, hidden_width):
    dh_node = lax.dot_general(
        d_y, w_out, (((1,), (1,)), ((), ())), preferred_element_type=jnp.float32
    )
    dz_node = (dh_node * swish_grad(z_node)).astype(jnp.bfloat16)
    return lax.dot_general(
        dz_node,
        w_in[hidden_width:, :],
        (((1,), (1,)), ((), ())),
        preferred_element_type=jnp.float32,
    )


def body(
    grid_lat,
    edge_lat,
    send_local,
    dest_band,
    receiver_in_band,
    mesh_lat,
    w_edge_in,
    w_edge_out,
    w_node_in,
    w_node_out,
    norm_gain,
    cotangent,
):
    band_count = lax.axis_size("band")
    edge_list = edge_lat.shape[0]
    hidden_width = edge_lat.shape[1]
    nodes = mesh_lat.shape[0]
    slot_capacity = max(2, 2 * edge_list // band_count)
    slot_count = band_count * slot_capacity
    x_in = (grid_lat[send_local].astype(jnp.float32) + edge_lat.astype(jnp.float32)).astype(
        jnp.bfloat16
    )
    target_band = dest_band[:, 0]
    band_hits = (target_band[:, None] == jnp.arange(band_count, dtype=jnp.int32)[None, :]).astype(
        jnp.int32
    )
    rank = jnp.sum(jnp.cumsum(band_hits, axis=0) * band_hits, axis=1) - 1
    slot_index = target_band * slot_capacity + rank
    slot_edge_index = (
        jnp.zeros((slot_count,), jnp.int32)
        .at[slot_index]
        .set(jnp.arange(edge_list, dtype=jnp.int32))
    )
    slot_valid_mask = jnp.zeros((slot_count,), jnp.bool_).at[slot_index].set(True)
    slot_target = (
        jnp.full((slot_count,), -1, jnp.int32)
        .at[slot_index]
        .set(receiver_in_band)
        .reshape(band_count, slot_capacity)
    )
    z_edge, h_edge, message = edge_forward(x_in, w_edge_in, w_edge_out)
    outgoing = jnp.where(
        slot_valid_mask[:, None], message[slot_edge_index], jnp.zeros((), jnp.bfloat16)
    )
    received_messages, received_target = (
        lax.all_to_all(
            outgoing.reshape(band_count, slot_capacity, hidden_width),
            "band",
            split_axis=0,
            concat_axis=0,
            tiled=True,
        ),
        lax.all_to_all(slot_target, "band", split_axis=0, concat_axis=0, tiled=True),
    )
    slot_message = received_messages.reshape(slot_count, hidden_width)
    target_nodes = received_target.reshape(slot_count)
    collect = (jnp.arange(nodes, dtype=jnp.int32)[:, None] == target_nodes[None, :]).astype(
        jnp.bfloat16
    )
    agg_part = jnp.dot(collect, slot_message, preferred_element_type=jnp.float32)
    agg = lax.psum(agg_part, "edge").astype(jnp.bfloat16)
    joined = jnp.concatenate([mesh_lat, agg], axis=1)
    z_node = jnp.dot(joined, w_node_in, preferred_element_type=jnp.float32)
    h_node = jax.nn.silu(z_node).astype(jnp.bfloat16)
    y_part = jnp.dot(h_node, w_node_out, preferred_element_type=jnp.float32)
    y_out = lax.psum(y_part.astype(jnp.bfloat16), "edge").astype(jnp.float32)
    new_mesh, d_y = norm_rows(y_out, mesh_lat, norm_gain, cotangent)
    dagg_part = node_backward(d_y, z_node, w_node_in, w_node_out, hidden_width)
    d_agg = lax.psum(dagg_part, "edge").astype(jnp.bfloat16)
    d_slot = lax.dot_general(
        collect, d_agg, (((0,), (0,)), ((), ())), preferred_element_type=jnp.float32
    ).astype(jnp.bfloat16)
    returned_gradient = lax.all_to_all(
        d_slot.reshape(band_count, slot_capacity, hidden_width),
        "band",
        split_axis=0,
        concat_axis=0,
        tiled=True,
    )
    message_gradient = returned_gradient.reshape(slot_count, hidden_width)[slot_index]
    grad_in, grad_out = edge_backward(x_in, z_edge, h_edge, message_gradient, w_edge_out)
    grad_edge_in, grad_edge_out = (
        lax.psum_scatter(grad_in, ("band", "edge"), scatter_dimension=0, tiled=True),
        lax.psum_scatter(grad_out, ("band", "edge"), scatter_dimension=0, tiled=True),
    )
    return (new_mesh, grad_edge_in, grad_edge_out)


def solution(mesh):
    in_specs = (
        P("band", None),
        P(("band", "edge"), None),
        P(("band", "edge")),
        P(("band", "edge"), None),
        P(("band", "edge")),
        P("band", None),
        P(),
        P(),
        P(None, "edge"),
        P("edge", None),
        P(),
        P("band", None),
    )
    out_specs = (P("band", None), P(("band", "edge"), None), P(("band", "edge"), None))
    return jax.shard_map(body, mesh=mesh, in_specs=in_specs, out_specs=out_specs, check_vma=False)
```

profile of v0, /device:TPU:1, one launch (start us, length us, event | category | flops | bytes accessed | tf_op | source)
XLA Modules:
  0.0 694.4 jit_solution(5950018871222052616)
XLA Ops:
  7.2 0.7 copy-done.8
  7.9 0.1 fusion.49
  8.0 0.2 reduce_window_sum.11
  8.2 0.2 select_reduce_fusion
  8.4 1.1 scatter_custom_fusion
  9.5 0.8 all_to_all.12
  10.3 20.7 %all-to-all-start = ((s32[128,1,2]{2,1,0:T(1,128)}), s32[128,1,2]{2,1,0:T(1,128)S(1)}, u32[]{:S(2)}, u32[]{:S(2)}) async-start(s32[128,1,2]{2,1,0:T(1,128)} %bitcast.3), calls=%async_computation | async-start | bytes 131072 | tf_op jit(solution)/shard_map/all_to_all | solution.py:114
  31.0 1.0 scatter_custom_fusion.2
  32.0 0.8 gather_fusion
  32.9 0.2 copy-done.3
  33.1 0.2 fusion.50
  33.3 0.8 copy-done.2
  34.1 0.3 convolution_convert_fusion.2
  34.4 1.2 gather_fusion.1
  35.6 0.1 gather.13
  35.7 1.0 scatter_custom_fusion.1
  36.7 0.2 broadcast_in_dim.45
  36.9 1.1 broadcast_select_fusion
  37.9 8.0 %all-to-all-done = s32[128,1,2]{2,1,0:T(1,128)S(1)} async-done(((s32[128,1,2]{2,1,0:T(1,128)}), s32[128,1,2]{2,1,0:T(1,128)S(1)}, u32[]{:S(2)}, u32[]{:S(2)}) %all-to-all-start) | async-done | bytes 1056 | tf_op jit(solution)/shard_map/all_to_all | solution.py:114
  46.0 8.2 %all-to-all-start.1 = ((bf16[128,2,512]{2,1,0:T(2,128)(2,1)}), bf16[128,2,512]{2,1,0:T(2,128)(2,1)S(1)}, u32[]{:S(2)}, u32[]{:S(2)}) async-start(bf16[128,2,512]{2,1,0:T(2,128)(2,1)} %broadcast_select_fusion), calls=%async_computation.1 | async-start | bytes 524288 | tf_op jit(solution)/shard_map/all_to_all | solution.py:107
  54.2 0.5 broadcast.106
  54.7 0.8 reduce.3
  55.5 0.1 eq.35
  55.7 21.0 %all-to-all-done.1 = bf16[128,2,512]{2,1,0:T(2,128)(2,1)S(1)} async-done(((bf16[128,2,512]{2,1,0:T(2,128)(2,1)}), bf16[128,2,512]{2,1,0:T(2,128)(2,1)S(1)}, u32[]{:S(2)}, u32[]{:S(2)}) %all-to-all-start.1) | async-done | bytes 262176 | tf_op jit(solution)/shard_map/all_to_all | solution.py:107
  76.6 0.1 reshape.59
  76.7 0.2 fusion.38
  77.0 18.7 %all-reduce.11 = bf16[256,512]{1,0:T(8,128)(2,1)S(1)} all-reduce(f32[256,512]{1,0:T(8,128)S(1)} %fusion.38), channel_id=1, replica_groups=mesh['band'=128,'edge'=4] {'edge'}, use_global_device_ids=true, to_apply=%region_5.6 | all-reduce | flops 131072 | bytes 786432 | tf_op jit(solution)/shard_map/psum | solution.py:122
  95.7 0.3 fusion.16
  96.0 0.6 copy-done.10
  96.6 0.9 convolution_convert_fusion.1
  97.6 49.1 %all-reduce.8.cloned.1.call-done = bf16[256,512]{1,0:T(8,128)(2,1)} async-done(((bf16[256,512]{1,0:T(8,128)(2,1)}), bf16[256,512]{1,0:T(8,128)(2,1)}) %all-reduce.8.cloned.1.call-update) | async-done | bytes 262160 | tf_op jit(solution)/shard_map/psum | solution.py:127
  146.7 1.1 convert_reduce_fusion
  147.8 0.2 fusion.15
  148.1 0.7 copy-done.7
  148.8 1.0 fusion.20
  149.7 1.6 fusion.3
  151.3 19.0 %all-reduce.12 = bf16[256,512]{1,0:T(8,128)(2,1)S(1)} all-reduce(f32[256,512]{1,0:T(8,128)S(1)} %fusion.3), channel_id=1, replica_groups=mesh['band'=128,'edge'=4] {'edge'}, use_global_device_ids=true, to_apply=%region_11.12 | all-reduce | flops 131072 | bytes 786432 | tf_op jit(solution)/shard_map/psum | solution.py:130
  170.4 0.3 convolution_convert_fusion
  170.7 0.8 reshape.60
  171.5 21.3 %all-to-all-start.2 = ((bf16[128,2,512]{2,1,0:T(2,128)(2,1)}), bf16[128,2,512]{2,1,0:T(2,128)(2,1)S(1)}, u32[]{:S(2)}, u32[]{:S(2)}) async-start(bf16[128,2,512]{2,1,0:T(2,128)(2,1)} %reshape.60), calls=%async_computation.2 | async-start | bytes 524288 | tf_op jit(solution)/shard_map/all_to_all | solution.py:134
  192.8 22.4 %all-to-all-done.2 = bf16[128,2,512]{2,1,0:T(2,128)(2,1)S(1)} async-done(((bf16[128,2,512]{2,1,0:T(2,128)(2,1)}), bf16[128,2,512]{2,1,0:T(2,128)(2,1)S(1)}, u32[]{:S(2)}, u32[]{:S(2)}) %all-to-all-start.2) | async-done | bytes 262176 | tf_op jit(solution)/shard_map/all_to_all | solution.py:134
  215.3 0.1 reshape.61
  215.4 0.8 gather_fusion.2
  216.2 1.5 fusion.1
  217.7 1.3 fusion.62
  219.1 465.9 %all-reduce.10.cloned.1.call-done = (f32[512,512]{1,0:T(8,128)}, f32[512,512]{1,0:T(8,128)}) async-done(((f32[512,512]{1,0:T(8,128)}, f32[512,512]{1,0:T(8,128)}), (f32[512,512]{1,0:T(8,128)}, f32[512,512]{1,0:T(8,128)})) %all-reduce.10.cloned.1.call-update) | async-done | bytes 2097168
  685.0 1.3 constant_dynamic-slice_fusion.1
  686.3 1.3 constant_dynamic-slice_fusion
  (36 shorter events, 0.3 us)
Async XLA Ops:
  7.2 24.8 %copy-start = (bf16[1024,512]{1,0:T(8,128)(2,1)S(1)}, bf16[1024,512]{1,0:T(8,128)(2,1)}, u32[]{:S(2)}) copy-start(bf16[1024,512]{1,0:T(8,128)(2,1)} %param.12) | copy-start | bytes 3145732
  7.2 0.7 copy-start.8
  10.2 20.7 %copy-start.11 = (s32[128]{0:T(128)S(1)}, s32[128]{0:T(128)}, u32[]{:S(2)}) copy-start(s32[128]{0:T(128)} %param.14) | copy-start | bytes 1540
  10.3 35.7 %all-to-all-start = ((s32[128,1,2]{2,1,0:T(1,128)}), s32[128,1,2]{2,1,0:T(1,128)S(1)}, u32[]{:S(2)}, u32[]{:S(2)}) async-start(s32[128,1,2]{2,1,0:T(1,128)} %bitcast.3), calls=%async_computation | async-start | bytes 131072 | tf_op jit(solution)/shard_map/all_to_all | solution.py:114
  32.0 1.0 copy-start.3
  32.0 1.1 copy-start.4
  33.1 1.0 copy-start.2
  46.0 30.7 %all-to-all-start.1 = ((bf16[128,2,512]{2,1,0:T(2,128)(2,1)}), bf16[128,2,512]{2,1,0:T(2,128)(2,1)S(1)}, u32[]{:S(2)}, u32[]{:S(2)}) async-start(bf16[128,2,512]{2,1,0:T(2,128)(2,1)} %broadcast_select_fusion), calls=%async_computation.1 | async-start | bytes 524288 | tf_op jit(solution)/shard_map/all_to_all | solution.py:107
  54.1 92.5 %all-reduce.8.cloned.1.call-start = ((), (), s32[]{:S(2)}) async-start(), calls=%async_computation.3 | async-start | bytes 524288 | tf_op jit(solution)/shard_map/psum | solution.py:127
  77.0 18.7 %copy-start.5 = (bf16[256,512]{1,0:T(8,128)(2,1)S(1)}, bf16[256,512]{1,0:T(8,128)(2,1)}, u32[]{:S(2)}) copy-start(bf16[256,512]{1,0:T(8,128)(2,1)} %param.17) | copy-start | bytes 786436
  77.0 18.7 %copy-start.9 = (bf16[1024,128]{1,0:T(8,128)(2,1)S(1)}, bf16[1024,128]{1,0:T(8,128)(2,1)}, u32[]{:S(2)}) copy-start(bf16[1024,128]{1,0:T(8,128)(2,1)} %param.20) | copy-start | bytes 786436
  95.7 0.9 copy-start.10
  96.6 0.9 copy-start.12
  146.7 1.2 copy-start.1
  146.7 1.4 copy-start.6
  148.1 0.7 copy-start.7
  171.5 43.8 %all-to-all-start.2 = ((bf16[128,2,512]{2,1,0:T(2,128)(2,1)}), bf16[128,2,512]{2,1,0:T(2,128)(2,1)S(1)}, u32[]{:S(2)}, u32[]{:S(2)}) async-start(bf16[128,2,512]{2,1,0:T(2,128)(2,1)} %reshape.60), calls=%async_computation.2 | async-start | bytes 524288 | tf_op jit(solution)/shard_map/all_to_all | solution.py:134
  192.8 492.2 %all-reduce.10.cloned.1.call-start = ((), (), s32[]{:S(2)}) async-start(), calls=%async_computation.4 | async-start | bytes 4194304
Sparse Core Ops, SparseCore 0:
  97.7 48.9 all-reduce.7
  219.2 465.7 all-reduce.9
where the time goes:
time: 695 us; the launch traced here: 694 us
  waiting for transfers between devices  566 us (81%)
  starting transfers between devices  50.3 us (7%)
  blocking collectives  37.7 us (5%)
  between operations  14.4 us (2%)
  local copies, waits for them, and re-layouts  14.3 us (2%)
    unnamed x3, waiting for transfers between devices  466 us
    psum x1, waiting for transfers between devices, body(): y_out = lax.psum(y_part.astype(jnp.bfloat16), 'edge').astype(jnp.float32)  49.1 us
    all_to_all x1, waiting for transfers between devices, body(): lax.all_to_all(d_slot.reshape(band_count, slot_capacity, hidden_width), '...  22.4 us
    all_to_all x1, starting transfers between devices, body(): lax.all_to_all(d_slot.reshape(band_count, slot_capacity, hidden_width), '...  21.3 us
    all_to_all x1, waiting for transfers between devices, body(): lax.all_to_all(outgoing.reshape(band_count, slot_capacity, hidden_width),...  21 us
    all_to_all x1, starting transfers between devices, body(): lax.all_to_all(slot_target, 'band', split_axis=0, concat_axis=0, tiled=True)  20.7 us
    psum x1, blocking collectives, body(): d_agg = lax.psum(dagg_part, 'edge').astype(jnp.bfloat16)  19 us
    psum x1, blocking collectives, body(): agg = lax.psum(agg_part, 'edge').astype(jnp.bfloat16)  18.7 us
  transfers between devices with their start and end apart: 5, of which 5 were waited for; matrix products, arithmetic and copies ran while one was open for 1% of the time, Pallas kernels for 0%

commit v1 on v0

v1 whole, which is shorter than its diff:
```python
import jax
import jax.numpy as jnp
from jax import lax
from jax.experimental import pallas as pl
from jax.experimental.pallas import tpu as pltpu
from jax.sharding import PartitionSpec as P

BF = jnp.bfloat16
F32 = jnp.float32
I32 = jnp.int32
MESH = pl.DeviceIdType.MESH

Z_AT = (0, 1, 15, 2, 14, 3, 13, 4, 12, 5, 11, 6, 10, 7, 9, 8)
Z_SEND = (8, 7, 9, 6, 10, 5, 11, 4, 12, 3, 13, 2, 14, 1, 15)
GROUPS = 4


def iota(shape, axis):
    return lax.broadcasted_iota(I32, shape, axis)


def one_hot(cond):
    return jnp.where(cond, 1.0, 0.0).astype(BF)


def mm(a, b):
    return jnp.dot(a, b, preferred_element_type=F32)


def mm_nt(a, b):
    return lax.dot_general(a, b, (((1,), (1,)), ((), ())), preferred_element_type=F32)


def mm_tn(a, b):
    return lax.dot_general(a, b, (((0,), (0,)), ((), ())), preferred_element_type=F32)


def row_order(shape, axis, x_first):
    p = iota(shape, axis)
    core, high, low, z = p >> 8, (p >> 6) & 3, (p >> 4) & 3, p & 15
    x, y = (high, low) if x_first else (low, high)
    return y * 128 + z * 8 + core * 4 + x


def kernel(
    grid_ref, edge_ref, send_ref, dest_ref, recv_ref, mesh_ref, wei_ref, weo_ref, wni_ref, wno_ref, gain_ref, cot_ref,
    new_ref, gin_ref, gout_ref,
    s1_src, s1_dst, c1_src, c1_dst, z_src, zc_src, zc_dst, xall, rx,
    wni, wno, sgrad, hid, nm,
    co_src, co_dst, ci_src, ci_dst, oy_src, oy_dst, ix_src, ix_dst, ox_src, ox_dst, iy_src, iy_dst,
    oz_src, oz_dst, iz_src, iz_dst, acc_o, acc_i, mid_o, mid_i,
    s_yc, s_yc_c, s_z, s_z_c, s_xf, s_rx, s_w, s_nm, s_core, s_r1, s_r2, s_rz,
):
    band = lax.axis_index("band")
    x = lax.axis_index("edge")
    y, z, c = band >> 5, (band >> 1) & 15, band & 1

    def at(ty, tz, tc, tx):
        return (((ty & 3) * 16 + (tz & 15)) * 2 + (tc & 1), tx & 3)

    def copy(src, dst, sems, i, target):
        return pltpu.make_async_remote_copy(
            src_ref=src, dst_ref=dst, send_sem=sems.at[0, i], recv_sem=sems.at[1, i],
            device_id=target, device_id_type=MESH,
        )

    barrier = pltpu.get_barrier_semaphore()
    greeted = [at(y, z + i, c, x) for i in Z_SEND]
    greeted += [at(y + i // 2, z, c + i % 2, x) for i in range(1, 8)]
    greeted += [at(y, z, c, x + i) for i in range(1, 4)]
    for other in greeted:
        pl.semaphore_signal(barrier, inc=1, device_id=other, device_id_type=MESH)

    eye = iota((128, 128), 0) == iota((128, 128), 1)
    dest = dest_ref[...]
    dest_b = jnp.broadcast_to(dest, (128, 128)).astype(F32)
    dest_col = jnp.sum(jnp.where(eye, dest_b, 0.0), axis=1, keepdims=True)
    earlier = (dest_col == dest_b) & (iota((128, 128), 0) < iota((128, 128), 1))
    rank = jnp.sum(jnp.where(earlier, 1.0, 0.0), axis=0, keepdims=True).astype(I32)
    slot = ((dest >> 5) * 2 + (dest & 1)) * 32 + ((dest >> 1) & 15) * 2 + rank
    code = ((dest * 2 + rank) * 256 + recv_ref[...]).astype(F32)
    send_b = jnp.broadcast_to(send_ref[...], (128, 128)).astype(F32)
    send_col = jnp.sum(jnp.where(eye, send_b, 0.0), axis=1, keepdims=True).astype(I32)
    pick = one_hot(send_col == iota((128, 1024), 1))
    x_in = (mm(pick, grid_ref[...]) + edge_ref[...].astype(F32)).astype(BF)
    order_in = one_hot(iota((512, 512), 1) == row_order((512, 512), 0, True))
    x_in = mm_nt(x_in, order_in).astype(BF)
    place = one_hot(iota((256, 128), 0) == slot)
    slots = mm(place, x_in).astype(BF)
    for i in range(8):
        s1_src[i] = slots[32 * i : 32 * (i + 1)]
    c1_src[...] = code

    pl.semaphore_wait(barrier, len(greeted))

    s1 = []
    for i in (4, 5, 2, 3, 6, 7, 1):
        ty, tc = y + i // 2, c + i % 2
        target = at(ty, z, tc, x)
        s1.append(copy(c1_src, c1_dst.at[i], s_yc_c, i, target))
        s1.append(copy(s1_src.at[(ty & 3) * 2 + (tc & 1)], s1_dst.at[i], s_yc, i, target))
    for d in s1:
        d.start()
    lanes = pl.ds(pl.multiple_of(x * 128, 128), 128)
    weights = []
    for i in (2, 1, 3):
        target = at(y, z, c, x + i)
        weights.append(copy(wni_ref, wni.at[:, lanes], s_w, i, target))
        weights.append(copy(wno_ref, wno.at[lanes, :], s_w, 4 + i, target))
    for d in weights:
        d.start()
    s1_dst[0] = s1_src[y * 2 + c]
    c1_dst[0] = c1_src[...]
    wni[:, lanes] = wni_ref[...]
    wno[lanes, :] = wno_ref[...]

    w_in = mm(order_in, wei_ref[...]).astype(BF)
    order_out = one_hot(iota((512, 512), 1) == row_order((512, 512), 0, False))
    w_out = mm(order_out, weo_ref[...]).astype(BF)
    o = iota((256, 256), 0)
    regroup = one_hot(iota((256, 256), 1) == (o & 7) * 32 + (o >> 4) * 2 + ((o >> 3) & 1))
    l = iota((256, 256), 1)
    to_rows = one_hot(iota((256, 256), 0) == ((l >> 3) & 1) * 128 + (l >> 4) * 8 + (l & 7))

    for d in s1:
        d.wait_recv()
    gathered = mm(regroup, s1_dst[...].reshape(256, 512)).astype(BF)
    for i in range(16):
        z_src[i] = gathered[16 * i : 16 * (i + 1)]
    zc_src[...] = jnp.concatenate([c1_dst[i] for i in range(8)], axis=0)
    s2 = {}
    for i in Z_SEND:
        p = Z_AT.index(i)
        target = at(y, z + i, c, x)
        s2[p] = (
            copy(zc_src, zc_dst.at[p], s_z_c, p, target),
            copy(z_src.at[(z + i) & 15], xall.at[0, p], s_z, p, target),
        )
        for d in s2[p]:
            d.start()
    xall[0, 0] = z_src[z]
    zc_dst[0] = zc_src[...]

    def edge_rows(plane, group):
        rows = xall[plane, pl.ds(4 * group, 4)].reshape(64, 512)
        z_edge = mm(rows, w_in)
        sig = jax.nn.sigmoid(z_edge)
        at_rows = pl.ds(plane * 256 + group * 64, 64)
        hid[at_rows, :] = (z_edge * sig).astype(BF)
        sgrad[at_rows, :] = sig * (1.0 + z_edge * (1.0 - sig))

    forward = []
    for g in range(GROUPS):
        for p in range(4 * g, 4 * g + 4):
            if p:
                for d in s2[p]:
                    d.wait_recv()
        part = pl.ds(4 * g, 4)
        sent = [copy(xall.at[0, part], xall.at[i, part], s_xf, g * 4 + i, at(y, z, c, x + i)) for i in (2, 1, 3)]
        for d in sent:
            d.start()
        forward.append(sent)
        edge_rows(0, g)

    codes = zc_dst[...].reshape(128, 128)
    found = []
    for r in range(2):
        off = codes - ((band * 2 + r) * 256).astype(F32)
        mine = jnp.where((off >= 0.0) & (off < 256.0), off + 1.0, 0.0).astype(BF)
        found.append(mm_nt(jnp.ones((8, 128), BF), mine))
    rx[0] = mm(jnp.concatenate(found, axis=1).astype(BF), to_rows)
    sent_rx = [copy(rx.at[0], rx.at[i], s_rx, i, at(y, z, c, x + i)) for i in (2, 1, 3)]
    for d in sent_rx:
        d.start()

    for d in weights:
        d.wait_recv()
    nodes = pl.ds(pl.multiple_of(x * 64, 64), 64)
    mesh = mesh_ref[nodes, :]
    z_mesh = mm(mesh, wni[0:512, :])
    w_bot = mm(order_out, wni[512:1024, :]).astype(BF)

    for g in range(GROUPS):
        for d in forward[g]:
            d.wait_recv()
        for plane in range(1, 4):
            edge_rows(plane, g)
    for d in sent_rx:
        d.wait_recv()

    node = iota((64, 256), 0).astype(F32) + (x * 64 + 1).astype(F32)
    collect = jnp.concatenate([one_hot(rx[i][0:1, :] == node) for i in range(4)], axis=1)
    agg_h = mm(collect, hid[...]).astype(BF)
    agg = mm_nt(agg_h, w_out).astype(BF)
    z_node = z_mesh + mm(agg, w_bot)
    sig = jax.nn.sigmoid(z_node)
    h_node = (z_node * sig).astype(BF)
    y_out = mm(h_node, wno[...])
    gain = gain_ref[...]
    mean_y = jnp.mean(y_out, axis=1, keepdims=True)
    centred = y_out - mean_y
    inv_std = lax.rsqrt(jnp.mean(centred * centred, axis=1, keepdims=True) + 1e-05)
    normed = centred * inv_std
    nm[nodes, :] = (mesh.astype(F32) + normed * gain).astype(BF)
    sent_nm = [copy(nm.at[nodes, :], nm.at[nodes, :], s_nm, i, at(y, z, c, x + i)) for i in (2, 1, 3)]
    for d in sent_nm:
        d.start()
    up = cot_ref[nodes, :].astype(F32) * gain
    d_y = (
        up - jnp.mean(up, axis=1, keepdims=True) - normed * jnp.mean(up * normed, axis=1, keepdims=True)
    ) * inv_std
    dh_node = mm_nt(d_y.astype(BF), wno[...])
    dz_node = (dh_node * (sig * (1.0 + z_node * (1.0 - sig)))).astype(BF)
    d_agg = mm_nt(dz_node, w_bot).astype(BF)
    dh = mm(d_agg, w_out).astype(BF)

    keep = pl.ds(pl.multiple_of(c * 256, 256), 256)
    give = pl.ds(pl.multiple_of((1 - c) * 256, 256), 256)
    other = at(y, z, c + 1, x)
    acc_o[...] = mm_tn(d_agg, agg_h)
    co_src[...] = acc_o[give, :].astype(BF)
    core_o = copy(co_src, co_dst, s_core, 0, other)
    core_o.start()
    d_edge = (mm_tn(collect, dh) * sgrad[...]).astype(BF)
    ci_src[...] = mm_tn(xall[:, :, :, give].reshape(1024, 256), d_edge).astype(BF)
    core_i = copy(ci_src, ci_dst, s_core, 1, other)
    core_i.start()

    core_o.wait_recv()
    acc_o[keep, :] += co_dst[...].astype(F32)
    oy_src[...] = acc_o[keep, :].astype(BF).reshape(4, 64, 512)
    sent_oy = [copy(oy_src.at[(y + i) & 3], oy_dst.at[i], s_r1, i, at(y + i, z, c, x)) for i in (2, 1, 3)]
    for d in sent_oy:
        d.start()
    acc_i[...] = mm_tn(xall[:, :, :, keep].reshape(1024, 256), d_edge)
    core_i.wait_recv()
    acc_i[...] += ci_dst[...].astype(F32)
    ix_src[...] = acc_i[...].astype(BF).reshape(4, 64, 512)
    sent_ix = [copy(ix_src.at[(x + i) & 3], ix_dst.at[i], s_r1, 4 + i, at(y, z, c, x + i)) for i in (2, 1, 3)]
    for d in sent_ix:
        d.start()

    for d in sent_oy:
        d.wait_recv()
    total = acc_o[pl.ds(pl.multiple_of(c * 256 + y * 64, 64), 64), :]
    for i in range(1, 4):
        total += oy_dst[i].astype(F32)
    mid_o[...] = total
    ox_src[...] = total.astype(BF).reshape(4, 16, 512)
    sent_ox = [copy(ox_src.at[(x + i) & 3], ox_dst.at[i], s_r2, i, at(y, z, c, x + i)) for i in (2, 1, 3)]
    for d in sent_ox:
        d.start()
    for d in sent_ix:
        d.wait_recv()
    total = acc_i[pl.ds(pl.multiple_of(x * 64, 64), 64), :]
    for i in range(1, 4):
        total += ix_dst[i].astype(F32)
    mid_i[...] = total
    iy_src[...] = total.astype(BF).reshape(4, 16, 512)
    sent_iy = [copy(iy_src.at[(y + i) & 3], iy_dst.at[i], s_r2, 4 + i, at(y + i, z, c, x)) for i in (2, 1, 3)]
    for d in sent_iy:
        d.start()

    def last(mid, here, sent, dst, src_z, dst_z, base):
        for d in sent:
            d.wait_recv()
        rows = mid[pl.ds(pl.multiple_of(here * 16, 16), 16), :]
        for i in range(1, 4):
            rows += dst[i].astype(F32)
        for i in range(16):
            src_z[i] = rows[i : i + 1]
        out = []
        for i in Z_SEND:
            out.append(copy(src_z.at[(z + i) & 15], dst_z.at[i], s_rz, base + i, at(y, z + i, c, x)))
            out[-1].start()
        return out

    sent_oz = last(mid_o, x, sent_ox, ox_dst, oz_src, oz_dst, 0)
    sent_iz = last(mid_i, y, sent_iy, iy_dst, iz_src, iz_dst, 16)

    for d in sent_nm:
        d.wait_recv()
    new_ref[...] = nm[...]

    def finish(sent, src_z, dst_z, out_ref):
        for d in sent:
            d.wait_recv()
        total = src_z[z]
        for i in range(1, 16):
            total += dst_z[i]
        out_ref[...] = total

    finish(sent_oz, oz_src, oz_dst, gout_ref)
    finish(sent_iz, iz_src, iz_dst, gin_ref)

    everything = s1 + weights + [d for pair in s2.values() for d in pair] + [d for sent in forward for d in sent]
    everything += sent_rx + sent_nm + [core_o, core_i] + sent_oy + sent_ix + sent_ox + sent_iy + sent_oz + sent_iz
    for d in everything:
        d.wait_send()


def body(
    grid_lat, edge_lat, send_local, dest_band, receiver_in_band, mesh_lat,
    w_edge_in, w_edge_out, w_node_in, w_node_out, norm_gain, cotangent,
):
    vmem = pl.BlockSpec(memory_space=pltpu.VMEM)
    dma = pltpu.SemaphoreType.DMA
    new_mesh, grad_in, grad_out = pl.pallas_call(
        kernel,
        out_shape=(
            jax.ShapeDtypeStruct((256, 512), BF),
            jax.ShapeDtypeStruct((1, 512), F32),
            jax.ShapeDtypeStruct((1, 512), F32),
        ),
        in_specs=[vmem] * 12,
        out_specs=(vmem, vmem, vmem),
        scratch_shapes=[
            pltpu.VMEM((8, 32, 512), BF), pltpu.VMEM((8, 32, 512), BF),
            pltpu.VMEM((1, 128), F32), pltpu.VMEM((8, 1, 128), F32),
            pltpu.VMEM((16, 16, 512), BF),
            pltpu.VMEM((8, 128), F32), pltpu.VMEM((16, 8, 128), F32),
            pltpu.VMEM((4, 16, 16, 512), BF), pltpu.VMEM((4, 8, 256), F32),
            pltpu.VMEM((1024, 512), BF), pltpu.VMEM((512, 512), BF),
            pltpu.VMEM((1024, 512), F32), pltpu.VMEM((1024, 512), BF), pltpu.VMEM((256, 512), BF),
            pltpu.VMEM((256, 512), BF), pltpu.VMEM((256, 512), BF),
            pltpu.VMEM((256, 512), BF), pltpu.VMEM((256, 512), BF),
            pltpu.VMEM((4, 64, 512), BF), pltpu.VMEM((4, 64, 512), BF),
            pltpu.VMEM((4, 64, 512), BF), pltpu.VMEM((4, 64, 512), BF),
            pltpu.VMEM((4, 16, 512), BF), pltpu.VMEM((4, 16, 512), BF),
            pltpu.VMEM((4, 16, 512), BF), pltpu.VMEM((4, 16, 512), BF),
            pltpu.VMEM((16, 1, 512), F32), pltpu.VMEM((16, 1, 512), F32),
            pltpu.VMEM((16, 1, 512), F32), pltpu.VMEM((16, 1, 512), F32),
            pltpu.VMEM((512, 512), F32), pltpu.VMEM((256, 512), F32),
            pltpu.VMEM((64, 512), F32), pltpu.VMEM((64, 512), F32),
            dma((2, 8)), dma((2, 8)), dma((2, 16)), dma((2, 16)), dma((2, 16)), dma((2, 4)),
            dma((2, 8)), dma((2, 4)), dma((2, 2)), dma((2, 8)), dma((2, 8)), dma((2, 32)),
        ],
        compiler_params=pltpu.CompilerParams(
            collective_id=0, has_side_effects=True, vmem_limit_bytes=48 * 2**20
        ),
        name="encoder_step",
    )(
        grid_lat, edge_lat, send_local.reshape(1, 128), dest_band.reshape(1, 128), receiver_in_band.reshape(1, 128),
        mesh_lat, w_edge_in, w_edge_out, w_node_in, w_node_out, norm_gain.reshape(1, 512), cotangent,
    )
    return new_mesh, grad_in, grad_out


def solution(mesh):
    in_specs = (
        P("band", None),
        P(("band", "edge"), None),
        P(("band", "edge")),
        P(("band", "edge"), None),
        P(("band", "edge")),
        P("band", None),
        P(),
        P(),
        P(None, "edge"),
        P("edge", None),
        P(),
        P("band", None),
    )
    out_specs = (P("band", None), P(("band", "edge"), None), P(("band", "edge"), None))
    return jax.shard_map(body, mesh=mesh, in_specs=in_specs, out_specs=out_specs, check_vma=False)
```

time: 695 us -> 84.9 us (0.12)
  waiting for transfers between devices: 566 us -> 0 us
  Pallas kernels: 0 us -> 73.3 us
  starting transfers between devices: 50.3 us -> 0 us
  blocking collectives: 37.7 us -> 0 us
  between operations: 14.4 us -> 0.69 us
    unnamed x3 -> x0, waiting for transfers between devices: 466 us -> none
    pallas_call x0 -> x1, Pallas kernels: none -> 73.3 us  [body(): pl.pallas_call(kernel, out_shape=(jax.ShapeDtypeStruct((256, 512), BF), j...]
    all_to_all x3 -> x0, waiting for transfers between devices: 51.4 us -> none  [the longest x1 22.4 us: body(): lax.all_to_all(d_slot.reshape(band_count, slot_capacity, hidden_width), '...]
    all_to_all x3 -> x0, starting transfers between devices: 50.2 us -> none  [the longest x1 21.3 us: body(): lax.all_to_all(d_slot.reshape(band_count, slot_capacity, hidden_width), '...]
    psum x1 -> x0, waiting for transfers between devices: 49.1 us -> none  [body(): y_out = lax.psum(y_part.astype(jnp.bfloat16), 'edge').astype(jnp.float32)]
    psum x2 -> x0, blocking collectives: 37.7 us -> none  [the longest x1 19 us: body(): d_agg = lax.psum(dagg_part, 'edge').astype(jnp.bfloat16)]
  transfers between devices with their start and end apart: 5 -> 0, of which waited for: 5 -> 0; matrix products, arithmetic and copies ran while one was open for 1% -> 0% of each run, Pallas kernels for 0% -> 0%
where the time goes in v1:
time: 84.9 us; the launch traced here: 84.5 us
  Pallas kernels  73.3 us (86%)
  local copies, waits for them, and re-layouts  10.5 us (12%)
    pallas_call x1, Pallas kernels, body(): pl.pallas_call(kernel, out_shape=(jax.ShapeDtypeStruct((256, 512), BF), j...  73.3 us
    unnamed x27, local copies, waits for them, and re-layouts  10.5 us

profile of v1, /device:TPU:1, one launch (start us, length us, event | category | flops | bytes accessed | tf_op | source)
XLA Modules:
  0.0 84.5 jit_solution(255164783107864358)
XLA Ops:
  0.6 0.0 copy-start.8
  0.6 0.0 copy-start.9
  0.7 0.0 copy-start.10
  0.7 0.0 copy-start.11
  0.7 0.6 copy-done.8
  1.3 0.0 copy-done.9
  1.3 0.0 copy-done.10
  1.3 0.0 copy-done.11
  1.3 0.0 copy-start
  1.3 1.2 %copy-done = bf16[1024,512]{1,0:T(8,128)(2,1)S(1)} copy-done((bf16[1024,512]{1,0:T(8,128)(2,1)S(1)}, bf16[1024,512]{1,0:T(8,128)(2,1)}, u32[]{:S(2)}) %copy-start) | copy-done | bytes 1048600
  2.6 0.0 copy-start.1
  2.6 1.0 %copy-done.1 = bf16[512,512]{1,0:T(8,128)(2,1)S(1)} copy-done((bf16[512,512]{1,0:T(8,128)(2,1)S(1)}, bf16[512,512]{1,0:T(8,128)(2,1)}, u32[]{:S(2)}) %copy-start.1) | copy-done | bytes 524312
  3.6 0.0 copy-start.2
  3.6 1.0 %copy-done.2 = bf16[512,512]{1,0:T(8,128)(2,1)S(1)} copy-done((bf16[512,512]{1,0:T(8,128)(2,1)S(1)}, bf16[512,512]{1,0:T(8,128)(2,1)}, u32[]{:S(2)}) %copy-start.2) | copy-done | bytes 524312
  4.6 0.0 copy-start.3
  4.7 0.9 %copy-done.3 = bf16[256,512]{1,0:T(8,128)(2,1)S(1)} copy-done((bf16[256,512]{1,0:T(8,128)(2,1)S(1)}, bf16[256,512]{1,0:T(8,128)(2,1)}, u32[]{:S(2)}) %copy-start.3) | copy-done | bytes 262168
  5.6 0.0 copy-start.4
  5.6 0.9 %copy-done.4 = bf16[1024,128]{1,0:T(8,128)(2,1)S(1)} copy-done((bf16[1024,128]{1,0:T(8,128)(2,1)S(1)}, bf16[1024,128]{1,0:T(8,128)(2,1)}, u32[]{:S(2)}) %copy-start.4) | copy-done | bytes 262168
  6.5 0.0 copy-start.5
  6.6 0.9 %copy-done.5 = bf16[256,512]{1,0:T(8,128)(2,1)S(1)} copy-done((bf16[256,512]{1,0:T(8,128)(2,1)S(1)}, bf16[256,512]{1,0:T(8,128)(2,1)}, u32[]{:S(2)}) %copy-start.5) | copy-done | bytes 262168
  7.5 0.0 copy-start.6
  7.5 0.9 %copy-done.6 = bf16[128,512]{1,0:T(8,128)(2,1)S(1)} copy-done((bf16[128,512]{1,0:T(8,128)(2,1)S(1)}, bf16[128,512]{1,0:T(8,128)(2,1)}, u32[]{:S(2)}) %copy-start.6) | copy-done | bytes 131096
  8.4 0.0 copy-start.7
  8.4 0.9 %copy-done.7 = bf16[128,512]{1,0:T(8,128)(2,1)S(1)} copy-done((bf16[128,512]{1,0:T(8,128)(2,1)S(1)}, bf16[128,512]{1,0:T(8,128)(2,1)}, u32[]{:S(2)}) %copy-start.7) | copy-done | bytes 131096
  9.3 73.3 %encoder_step.1 = (bf16[256,512]{1,0:T(8,128)(2,1)S(1)}, f32[1,512]{1,0:T(1,128)S(1)}, f32[1,512]{1,0:T(1,128)S(1)}) custom-call(bf16[1024,512]{1,0:T(8,128)(2,1)S(1)} %copy-done, bf16[128,512]{1,0:T(8,128)(2,1)S(1)} %copy-done.6, s32[1,128]{1,0:T(1,128)S(1)} %bitcast.5, s32[1,128]{1,0:T(1,128)S(1)} %bitcast.6, s32[1,128]{1,0:T(1,128)S(1)} %bitcast.7, ...), custom_call_target="tpu_custom_call" | custom-call | tf_op jit(solution)/shard_map/encoder_step/pallas_call | solution.py:308
  82.6 0.7 copy.18
  83.3 0.6 copy.19
  83.9 0.6 copy.20
Async XLA Ops:
  0.6 0.7 copy-start.8
  0.6 0.7 copy-start.9
  0.7 0.7 copy-start.10
  0.7 0.7 copy-start.11
  1.3 1.2 %copy-start = (bf16[1024,512]{1,0:T(8,128)(2,1)S(1)}, bf16[1024,512]{1,0:T(8,128)(2,1)}, u32[]{:S(2)}) copy-start(bf16[1024,512]{1,0:T(8,128)(2,1)} %grid_ref.1) | copy-start | bytes 3145732
  2.6 1.0 %copy-start.1 = (bf16[512,512]{1,0:T(8,128)(2,1)S(1)}, bf16[512,512]{1,0:T(8,128)(2,1)}, u32[]{:S(2)}) copy-start(bf16[512,512]{1,0:T(8,128)(2,1)} %wei_ref.1) | copy-start | bytes 1572868
  3.6 1.0 %copy-start.2 = (bf16[512,512]{1,0:T(8,128)(2,1)S(1)}, bf16[512,512]{1,0:T(8,128)(2,1)}, u32[]{:S(2)}) copy-start(bf16[512,512]{1,0:T(8,128)(2,1)} %weo_ref.1) | copy-start | bytes 1572868
  4.6 0.9 %copy-start.3 = (bf16[256,512]{1,0:T(8,128)(2,1)S(1)}, bf16[256,512]{1,0:T(8,128)(2,1)}, u32[]{:S(2)}) copy-start(bf16[256,512]{1,0:T(8,128)(2,1)} %mesh_ref.1) | copy-start | bytes 786436
  5.6 0.9 %copy-start.4 = (bf16[1024,128]{1,0:T(8,128)(2,1)S(1)}, bf16[1024,128]{1,0:T(8,128)(2,1)}, u32[]{:S(2)}) copy-start(bf16[1024,128]{1,0:T(8,128)(2,1)} %wni_ref.1) | copy-start | bytes 786436
  6.5 0.9 %copy-start.5 = (bf16[256,512]{1,0:T(8,128)(2,1)S(1)}, bf16[256,512]{1,0:T(8,128)(2,1)}, u32[]{:S(2)}) copy-start(bf16[256,512]{1,0:T(8,128)(2,1)} %cot_ref.1) | copy-start | bytes 786436
  7.5 0.9 %copy-start.6 = (bf16[128,512]{1,0:T(8,128)(2,1)S(1)}, bf16[128,512]{1,0:T(8,128)(2,1)}, u32[]{:S(2)}) copy-start(bf16[128,512]{1,0:T(8,128)(2,1)} %edge_ref.1) | copy-start | bytes 393220
  8.4 0.9 %copy-start.7 = (bf16[128,512]{1,0:T(8,128)(2,1)S(1)}, bf16[128,512]{1,0:T(8,128)(2,1)}, u32[]{:S(2)}) copy-start(bf16[128,512]{1,0:T(8,128)(2,1)} %wno_ref.1) | copy-start | bytes 393220

commit v2 on v1

v2 whole, which is shorter than its diff:
```python
import jax
import jax.numpy as jnp
from jax import lax
from jax.experimental import pallas as pl
from jax.experimental.pallas import tpu as pltpu
from jax.sharding import PartitionSpec as P

BF = jnp.bfloat16
F32 = jnp.float32
I32 = jnp.int32
MESH = pl.DeviceIdType.MESH

Z_AT = (0, 1, 15, 2, 14, 3, 13, 4, 12, 5, 11, 6, 10, 7, 9, 8)
Z_LAST = Z_AT[:0:-1]
GROUPS = ((0, 4), (4, 4), (8, 4), (12, 2), (14, 2))


def iota(shape, axis):
    return lax.broadcasted_iota(I32, shape, axis)


def one_hot(cond):
    return jnp.where(cond, 1.0, 0.0).astype(BF)


def mm(a, b):
    return jnp.dot(a, b, preferred_element_type=F32)


def mm_nt(a, b):
    return lax.dot_general(a, b, (((1,), (1,)), ((), ())), preferred_element_type=F32)


def mm_tn(a, b):
    return lax.dot_general(a, b, (((0,), (0,)), ((), ())), preferred_element_type=F32)


def sigmoid(v):
    return 0.5 * jnp.tanh(0.5 * v) + 0.5


def row_order(shape, axis, x):
    p = iota(shape, axis)
    return ((p >> 4) & 3) * 128 + (p & 15) * 8 + (p >> 6) * 4 + x


def kernel(
    grid_hbm, edge_hbm, send_hbm, dest_hbm, recv_hbm, mesh_hbm, wei_hbm, weo_hbm, wni_hbm, wno_hbm, gain_hbm, cot_hbm,
    new_hbm, gin_ref, gout_ref,
    s1_src, s1_dst, c1_src, c1_dst, z_src, r_src, xall, rx, xt, ct, wni, wno, sgrad, hid, nm,
    core_src, core_dst, y_src, y_dst, last_src, last_dst, acc,
    grid_ref, edge_ref, send_ref, dest_ref, recv_ref, mesh_ref, wei_ref, weo_ref, gain_ref, cot_ref,
    s_in, s_out, s_yc, s_yc_c, s_z, s_z_r, s_xf, s_rx, s_w, s_sh, s_core, s_y, s_last,
):
    band = lax.axis_index("band")
    x = lax.axis_index("edge")
    y, z, c = band >> 5, (band >> 1) & 15, band & 1

    def at(ty, tz, tc, tx):
        return (((ty & 3) * 16 + (tz & 15)) * 2 + (tc & 1), tx & 3)

    def copy(src, dst, sems, i, target):
        return pltpu.make_async_remote_copy(
            src_ref=src, dst_ref=dst, send_sem=sems.at[0, i], recv_sem=sems.at[1, i],
            device_id=target, device_id_type=MESH,
        )

    started, landed = [], set()

    def go(copies):
        for d in copies:
            d.start()
            started.append(d)
        return copies

    def got(copies):
        for d in copies:
            d.wait_recv()
            landed.add(id(d))

    def finish_all():
        for d in started:
            if id(d) not in landed:
                d.wait_recv()
        for d in started:
            d.wait_send()

    barrier = pltpu.get_barrier_semaphore()
    greeted = [at(y, z + i, c, x) for i in Z_AT[1:]]
    greeted += [at(y + i // 2, z, c + i % 2, x) for i in range(1, 8)]
    greeted += [at(y, z, c, x + i) for i in range(1, 4)]
    for other in greeted:
        pl.semaphore_signal(barrier, inc=1, device_id=other, device_id_type=MESH)

    lanes = pl.ds(pl.multiple_of(x * 128, 128), 128)
    half = pl.ds(pl.multiple_of(c * 512, 512), 512)

    def quarter(i):
        return pl.ds(pl.multiple_of((i & 3) * 128 + c * 64, 64), 64)

    piece = pl.ds(pl.multiple_of(c * 64, 64), 64)
    loads = {}
    for src, dst in (
        (dest_hbm, dest_ref), (send_hbm, send_ref), (recv_hbm, recv_ref), (grid_hbm, grid_ref), (edge_hbm, edge_ref),
        (wei_hbm, wei_ref), (weo_hbm, weo_ref), (wni_hbm.at[half, :], wni.at[half, lanes]),
        (wno_hbm.at[piece, :], wno.at[quarter(x), :]), (mesh_hbm, mesh_ref), (gain_hbm, gain_ref),
        (cot_hbm, cot_ref),
    ):
        i = len(loads)
        loads[i] = pltpu.make_async_copy(src, dst, s_in.at[i])
        loads[i].start()

    def loaded(*which):
        for i in which:
            loads[i].wait()

    loaded(0, 1, 2)
    eye = iota((128, 128), 0) == iota((128, 128), 1)
    dest = dest_ref[...]
    dest_b = jnp.broadcast_to(dest, (128, 128)).astype(F32)
    dest_col = jnp.sum(jnp.where(eye, dest_b, 0.0), axis=1, keepdims=True)
    earlier = (dest_col == dest_b) & (iota((128, 128), 0) < iota((128, 128), 1))
    rank = jnp.sum(jnp.where(earlier, 1.0, 0.0), axis=0, keepdims=True).astype(I32)
    slot = ((dest >> 5) * 2 + (dest & 1)) * 32 + ((dest >> 1) & 15) * 2 + rank
    code = ((dest * 2 + rank) * 256 + recv_ref[...]).astype(F32)
    send_b = jnp.broadcast_to(send_ref[...], (128, 128)).astype(F32)
    send_col = jnp.sum(jnp.where(eye, send_b, 0.0), axis=1, keepdims=True).astype(I32)
    pick = one_hot(send_col == iota((128, 1024), 1))
    loaded(3, 4)
    x_in = (mm(pick, grid_ref[...]) + edge_ref[...].astype(F32)).astype(BF)
    place = one_hot(iota((256, 128), 0) == slot)
    slots = mm(place, x_in).astype(BF)
    for i in range(8):
        s1_src[i] = slots[32 * i : 32 * (i + 1)]
    c1_src[...] = code

    pl.semaphore_wait(barrier, len(greeted))

    s1, s1_codes = [], []
    for i in (4, 5, 2, 3, 6, 7, 1):
        s1_codes.append(copy(c1_src, c1_dst.at[i], s_yc_c, i, at(y + i // 2, z, c + i % 2, x)))
    go(s1_codes)
    for i in (4, 5, 2, 3, 6, 7, 1):
        ty, tc = y + i // 2, c + i % 2
        s1.append(copy(s1_src.at[(ty & 3) * 2 + (tc & 1)], s1_dst.at[i], s_yc, i, at(ty, z, tc, x)))
    go(s1)
    weights = []
    for i in (2, 1, 3):
        target = at(y, z, c, x + i)
        weights.append(copy(wni_hbm.at[half, :], wni.at[half, lanes], s_w, i, target))
        weights.append(copy(wno_hbm.at[piece, :], wno.at[quarter(x), :], s_w, 4 + i, target))
    go(weights)
    s1_dst[0] = s1_src[y * 2 + c]
    c1_dst[0] = c1_src[...]

    o, lane = iota((256, 256), 0), iota((256, 256), 1)
    regroup = one_hot(lane == (o & 7) * 32 + (o >> 4) * 2 + ((o >> 3) & 1))
    ones = jnp.ones((128, 128), BF)
    chunk_of = one_hot(iota((16, 256), 0) == iota((16, 256), 1) >> 4)
    o, lane = iota((256, 128), 0), iota((256, 128), 1)
    in_chunk = lane == (o & 15)
    slot_code = ((((y * 16 + (o >> 4)) * 2 + c) * 2 + ((o >> 3) & 1)) * 256).astype(F32)

    got(s1_codes)
    codes = jnp.concatenate([c1_dst[i] for i in range(8)], axis=0)
    off = jnp.broadcast_to(codes[None], (32, 8, 128)).reshape(256, 128) - slot_code
    found = mm(jnp.where((off >= 0.0) & (off < 256.0), off + 1.0, 0.0).astype(BF), ones)
    found = mm(chunk_of, jnp.where(in_chunk, found, 0.0).astype(BF))
    for i in range(16):
        r_src[i] = found[i : i + 1]
    s2, s2_r = {}, {}
    for p in range(1, 16):
        i = Z_AT[p]
        s2_r[p] = copy(r_src.at[(z + i) & 15], rx.at[0, p], s_z_r, p, at(y, z + i, c, x))
        go([s2_r[p]])

    got(s1)
    gathered = mm(regroup, s1_dst[...].reshape(256, 512)).astype(BF)
    for i in range(16):
        z_src[i] = gathered[16 * i : 16 * (i + 1)]
    for p in range(1, 16):
        i = Z_AT[p]
        s2[p] = copy(z_src.at[(z + i) & 15], xall.at[0, p], s_z, p, at(y, z + i, c, x))
        go([s2[p]])
    xall[0, 0] = z_src[z]
    rx[0, 0] = r_src[z]

    loaded(5, 6)
    order = one_hot(iota((128, 512), 1) == row_order((128, 512), 0, x))

    def edge_rows(first, planes, begin, count):
        n = planes * count * 16
        rows = xall[first : first + planes, begin : begin + count].reshape(n, 512)
        z_edge = mm(rows, wei_ref[...])
        sig = sigmoid(z_edge)
        at_rows = pl.ds((begin * 4 + first * count) * 16, n)
        hid[at_rows, :] = (z_edge * sig).astype(BF)
        sgrad[at_rows, :] = sig * (1.0 + z_edge * (1.0 - sig))

    def turn_rows(begin, count):
        xt[:, begin * 64 : (begin + count) * 64] = mm_nt(
            order, xall[:, begin : begin + count].reshape(count * 64, 512)
        ).astype(BF)

    def collect(begin, count):
        n = count * 64
        rows = jnp.concatenate([rx[k, p] for k in range(4) for p in range(begin, begin + count)], axis=0)
        spread = one_hot(iota((n, 4 * count), 0) >> 4 == iota((n, 4 * count), 1))
        where = jnp.where(iota((n, 128), 1) == (iota((n, 128), 0) & 15), mm(spread, rows.astype(BF)), 0.0)
        where = mm(where.astype(BF), jnp.ones((128, 256), BF))
        hit = one_hot(where == (iota((n, 256), 1) + 1).astype(F32))
        ct[begin * 64 : begin * 64 + n, :] = hit
        return mm_tn(hit, hid[begin * 64 : begin * 64 + n, :])

    forward = []
    for begin, count in GROUPS:
        new = [p for p in range(begin, begin + count) if p]
        got([s2[p] for p in new])
        got([s2_r[p] for p in new])
        part = pl.ds(begin, count)
        sent = [copy(xall.at[0, part], xall.at[i, part], s_xf, begin * 4 + i, at(y, z, c, x + i)) for i in (2, 1, 3)]
        sent += [copy(rx.at[0, part], rx.at[i, part], s_rx, begin * 4 + i, at(y, z, c, x + i)) for i in (2, 1, 3)]
        forward.append(go(sent))
        edge_rows(0, 1, begin, count)
        if begin == GROUPS[1][0]:
            got(weights)
            loaded(7, 8)
            other = at(y, z, c + 1, x)
            shared = [copy(wni.at[half, :], wni.at[half, :], s_sh, 0, other)]
            for i in range(4):
                shared.append(copy(wno.at[quarter(i), :], wno.at[quarter(i), :], s_sh, 1 + i, other))
            go(shared)
        if begin == GROUPS[3][0]:
            got(shared)
            loaded(9, 10, 11)
            mesh = mesh_ref[...]
            z_mesh = mm(mesh, wni[0:512, :])
            w_both = mm_tn(weo_ref[...], wni[512:1024, :]).astype(BF)
            w_turn = mm(order, wni[512:1024, :]).astype(BF)

    agg_h = jnp.zeros((256, 512), F32)
    for (begin, count), sent in zip(GROUPS, forward):
        got(sent)
        edge_rows(1, 3, begin, count)
        agg_h += collect(begin, count)
        if begin < GROUPS[-1][0]:
            turn_rows(begin, count)

    agg_h = agg_h.astype(BF)
    z_node = z_mesh + mm(agg_h, w_both)
    sig = sigmoid(z_node)
    h_node = (z_node * sig).astype(BF)
    y_out = mm(h_node, wno[...])
    gain = gain_ref[...]
    mean_y = jnp.mean(y_out, axis=1, keepdims=True)
    centred = y_out - mean_y
    inv_std = lax.rsqrt(jnp.mean(centred * centred, axis=1, keepdims=True) + 1e-05)
    normed = centred * inv_std
    up = cot_ref[...].astype(F32) * gain
    d_y = (
        up - jnp.mean(up, axis=1, keepdims=True) - normed * jnp.mean(up * normed, axis=1, keepdims=True)
    ) * inv_std
    dh_node = mm_nt(d_y.astype(BF), wno[...])
    dz_node = (dh_node * (sig * (1.0 + z_node * (1.0 - sig)))).astype(BF)
    dh = mm_nt(dz_node, w_both).astype(BF)
    d_agg = mm_nt(dz_node, w_turn).astype(BF)

    turn_rows(*GROUPS[-1])
    d_edge = (mm(ct[...], dh) * sgrad[...]).astype(BF)
    acc[0] = mm(xt[...], d_edge)
    acc[1] = mm_tn(d_agg, agg_h)
    keep = pl.ds(pl.multiple_of(c * 64, 64), 64)
    give = pl.ds(pl.multiple_of((1 - c) * 64, 64), 64)
    core_src[...] = acc[:, give, :].astype(BF)
    to_core = go([copy(core_src, core_dst, s_core, 0, other)])
    nm[...] = (mesh.astype(F32) + normed * gain).astype(BF)
    stored = pltpu.make_async_copy(nm, new_hbm, s_out)
    stored.start()

    got(to_core)
    acc[:, keep, :] += core_dst[...].astype(F32)
    for i in range(4):
        y_src[i] = acc[:, pl.ds(pl.multiple_of(c * 64 + i * 16, 16), 16), :].astype(BF)
    to_y = go([copy(y_src.at[(y + i) & 3], y_dst.at[i], s_y, i, at(y + i, z, c, x)) for i in (2, 1, 3)])
    got(to_y)
    rows = acc[:, pl.ds(pl.multiple_of(c * 64 + y * 16, 16), 16), :]
    for i in range(1, 4):
        rows += y_dst[i].astype(F32)
    for i in range(16):
        last_src[i, 0] = rows[0, i : i + 1]
        last_src[i, 1] = rows[1, i : i + 1]
    to_z = []
    for i in Z_LAST:
        to_z += go([copy(last_src.at[(z + i) & 15], last_dst.at[i], s_last, i, at(y, z + i, c, x))])
    total = last_src[z]
    for i in Z_AT[1:]:
        got([to_z[Z_LAST.index(i)]])
        total += last_dst[i]
    gin_ref[...] = total[0]
    gout_ref[...] = total[1]
    stored.wait()
    finish_all()


def body(
    grid_lat, edge_lat, send_local, dest_band, receiver_in_band, mesh_lat,
    w_edge_in, w_edge_out, w_node_in, w_node_out, norm_gain, cotangent,
):
    vmem = pl.BlockSpec(memory_space=pltpu.VMEM)
    dma = pltpu.SemaphoreType.DMA
    new_mesh, grad_in, grad_out = pl.pallas_call(
        kernel,
        out_shape=(
            jax.ShapeDtypeStruct((256, 512), BF),
            jax.ShapeDtypeStruct((1, 512), F32),
            jax.ShapeDtypeStruct((1, 512), F32),
        ),
        in_specs=[pl.BlockSpec(memory_space=pl.ANY)] * 12,
        out_specs=(pl.BlockSpec(memory_space=pl.ANY), vmem, vmem),
        scratch_shapes=[
            pltpu.VMEM((8, 32, 512), BF), pltpu.VMEM((8, 32, 512), BF),
            pltpu.VMEM((1, 128), F32), pltpu.VMEM((8, 1, 128), F32),
            pltpu.VMEM((16, 16, 512), BF), pltpu.VMEM((16, 1, 128), F32),
            pltpu.VMEM((4, 16, 16, 512), BF), pltpu.VMEM((4, 16, 1, 128), F32),
            pltpu.VMEM((128, 1024), BF), pltpu.VMEM((1024, 256), BF),
            pltpu.VMEM((1024, 512), BF), pltpu.VMEM((512, 512), BF),
            pltpu.VMEM((1024, 512), F32), pltpu.VMEM((1024, 512), BF), pltpu.VMEM((256, 512), BF),
            pltpu.VMEM((2, 64, 512), BF), pltpu.VMEM((2, 64, 512), BF),
            pltpu.VMEM((4, 2, 16, 512), BF), pltpu.VMEM((4, 2, 16, 512), BF),
            pltpu.VMEM((16, 2, 1, 512), F32), pltpu.VMEM((16, 2, 1, 512), F32), pltpu.VMEM((2, 128, 512), F32),
            pltpu.VMEM((1024, 512), BF), pltpu.VMEM((128, 512), BF),
            pltpu.VMEM((1, 128), I32), pltpu.VMEM((1, 128), I32), pltpu.VMEM((1, 128), I32),
            pltpu.VMEM((256, 512), BF), pltpu.VMEM((512, 512), BF), pltpu.VMEM((512, 512), BF),
            pltpu.VMEM((1, 512), F32), pltpu.VMEM((256, 512), BF),
            dma((12,)), dma, dma((2, 8)), dma((2, 8)), dma((2, 16)), dma((2, 16)), dma((2, 64)), dma((2, 64)),
            dma((2, 8)), dma((2, 5)), dma((2, 1)), dma((2, 4)), dma((2, 16)),
        ],
        compiler_params=pltpu.CompilerParams(
            collective_id=0, has_side_effects=True, vmem_limit_bytes=56 * 2**20
        ),
        name="encoder_step",
    )(
        grid_lat, edge_lat, send_local.reshape(1, 128), dest_band.reshape(1, 128), receiver_in_band.reshape(1, 128),
        mesh_lat, w_edge_in, w_edge_out, w_node_in, w_node_out, norm_gain.reshape(1, 512), cotangent,
    )
    return new_mesh, grad_in, grad_out


def solution(mesh):
    in_specs = (
        P("band", None),
        P(("band", "edge"), None),
        P(("band", "edge")),
        P(("band", "edge"), None),
        P(("band", "edge")),
        P("band", None),
        P(),
        P(),
        P(None, "edge"),
        P("edge", None),
        P(),
        P("band", None),
    )
    out_specs = (P("band", None), P(("band", "edge"), None), P(("band", "edge"), None))
    return jax.shard_map(body, mesh=mesh, in_specs=in_specs, out_specs=out_specs, check_vma=False)
```

time: 84.9 us -> 66 us (0.78)
  Pallas kernels: 73.3 us -> 62.2 us
  local copies, waits for them, and re-layouts: 10.5 us -> 2.93 us
    pallas_call x1, Pallas kernels: 73.3 us -> 62.2 us  [body(): pl.pallas_call(kernel, out_shape=(jax.ShapeDtypeStruct((256, 512), BF), j...]
    unnamed x27 -> x7, local copies, waits for them, and re-layouts: 10.5 us -> 2.93 us
where the time goes in v2:
time: 66 us; the launch traced here: 65.8 us
  Pallas kernels  62.2 us (94%)
  local copies, waits for them, and re-layouts  2.93 us (4%)
    pallas_call x1, Pallas kernels, body(): pl.pallas_call(kernel, out_shape=(jax.ShapeDtypeStruct((256, 512), BF), j...  62.2 us
    unnamed x7, local copies, waits for them, and re-layouts  2.93 us

profile of v2, /device:TPU:1, one launch (start us, length us, event | category | flops | bytes accessed | tf_op | source)
XLA Modules:
  0.0 65.8 jit_solution(8194287419487224752)
XLA Ops:
  0.6 62.2 %encoder_step.1 = (bf16[256,512]{1,0:T(8,128)(2,1)}, f32[1,512]{1,0:T(1,128)}, f32[1,512]{1,0:T(1,128)}) custom-call(bf16[1024,512]{1,0:T(8,128)(2,1)} %grid_hbm.1, bf16[128,512]{1,0:T(8,128)(2,1)} %edge_hbm.1, s32[1,128]{1,0:T(1,128)} %bitcast.5, s32[1,128]{1,0:T(1,128)} %bitcast.6, s32[1,128]{1,0:T(1,128)} %bitcast.7, bf16[256,512]{1,0:T(8,128)(2,1)} %mesh_hbm.1, ...), custom_call_target="tpu_custom_call" | custom-call | tf_op jit(solution)/shard_map/encoder_step/pallas_call | solution.py:311
  62.9 0.0 copy-start.1
  62.9 1.7 %copy.18 = bf16[256,512]{1,0:T(8,128)(2,1)} copy(bf16[256,512]{1,0:T(8,128)(2,1)} %get-tuple-element.6) | data formatting | bytes 524288
  64.6 0.0 copy-done.1
  64.6 0.0 copy-start
  64.6 0.6 copy.19
  65.1 0.1 copy-done
  65.2 0.6 copy.20
Async XLA Ops:
  62.9 1.7 %copy-start.1 = (f32[1,512]{1,0:T(1,128)S(1)}, f32[1,512]{1,0:T(1,128)}, u32[]{:S(2)}) copy-start(f32[1,512]{1,0:T(1,128)} %get-tuple-element.7) | copy-start | bytes 6148
  64.6 0.7 %copy-start = (f32[1,512]{1,0:T(1,128)S(1)}, f32[1,512]{1,0:T(1,128)}, u32[]{:S(2)}) copy-start(f32[1,512]{1,0:T(1,128)} %get-tuple-element.8) | copy-start | bytes 6148

commit v3 on v2

--- a/solution.py
+++ b/solution.py
@@ -12,7 +12,7 @@
 
 Z_AT = (0, 1, 15, 2, 14, 3, 13, 4, 12, 5, 11, 6, 10, 7, 9, 8)
 Z_LAST = Z_AT[:0:-1]
-GROUPS = ((0, 4), (4, 4), (8, 4), (12, 2), (14, 2))
+GROUPS = ((0, 4), (4, 4), (8, 2), (10, 2), (12, 2), (14, 2))
 
 
 def iota(shape, axis):
@@ -86,7 +86,7 @@
             d.wait_send()
 
     barrier = pltpu.get_barrier_semaphore()
-    greeted = [at(y, z + i, c, x) for i in Z_AT[1:]]
+    greeted = [at(y, z + i, c, x) for i in Z_LAST]
     greeted += [at(y + i // 2, z, c + i % 2, x) for i in range(1, 8)]
     greeted += [at(y, z, c, x + i) for i in range(1, 4)]
     for other in greeted:
@@ -237,6 +237,11 @@
             z_mesh = mm(mesh, wni[0:512, :])
             w_both = mm_tn(weo_ref[...], wni[512:1024, :]).astype(BF)
             w_turn = mm(order, wni[512:1024, :]).astype(BF)
+            w_last = wno[...].astype(F32)
+            w_flat = (w_last - jnp.mean(w_last, axis=1, keepdims=True)).astype(BF)
+            gain = gain_ref[...]
+            up = cot_ref[...].astype(F32) * gain
+            up = up - jnp.mean(up, axis=1, keepdims=True)
 
     agg_h = jnp.zeros((256, 512), F32)
     for (begin, count), sent in zip(GROUPS, forward):
@@ -247,23 +252,22 @@
             turn_rows(begin, count)
 
     agg_h = agg_h.astype(BF)
-    z_node = z_mesh + mm(agg_h, w_both)
-    sig = sigmoid(z_node)
-    h_node = (z_node * sig).astype(BF)
-    y_out = mm(h_node, wno[...])
-    gain = gain_ref[...]
-    mean_y = jnp.mean(y_out, axis=1, keepdims=True)
-    centred = y_out - mean_y
-    inv_std = lax.rsqrt(jnp.mean(centred * centred, axis=1, keepdims=True) + 1e-05)
-    normed = centred * inv_std
-    up = cot_ref[...].astype(F32) * gain
-    d_y = (
-        up - jnp.mean(up, axis=1, keepdims=True) - normed * jnp.mean(up * normed, axis=1, keepdims=True)
-    ) * inv_std
-    dh_node = mm_nt(d_y.astype(BF), wno[...])
-    dz_node = (dh_node * (sig * (1.0 + z_node * (1.0 - sig)))).astype(BF)
-    dh = mm_nt(dz_node, w_both).astype(BF)
-    d_agg = mm_nt(dz_node, w_turn).astype(BF)
+    halves = (slice(0, 128), slice(128, 256))
+    z_node = [z_mesh[h] + mm(agg_h[h], w_both) for h in halves]
+    sig = [sigmoid(v) for v in z_node]
+    h_node = [(v * s).astype(BF) for v, s in zip(z_node, sig)]
+    centred = [mm(v, w_flat) for v in h_node]
+    inv_std = [lax.rsqrt(jnp.mean(v * v, axis=1, keepdims=True) + 1e-05) for v in centred]
+    normed = [v * s for v, s in zip(centred, inv_std)]
+    d_y = [
+        ((up[h] - v * jnp.mean(up[h] * v, axis=1, keepdims=True)) * s).astype(BF)
+        for h, v, s in zip(halves, normed, inv_std)
+    ]
+    dz_node = [
+        (mm_nt(d, wno[...]) * (s * (1.0 + v * (1.0 - s)))).astype(BF) for d, s, v in zip(d_y, sig, z_node)
+    ]
+    dh = jnp.concatenate([mm_nt(d, w_both).astype(BF) for d in dz_node], axis=0)
+    d_agg = jnp.concatenate([mm_nt(d, w_turn).astype(BF) for d in dz_node], axis=0)
 
     turn_rows(*GROUPS[-1])
     d_edge = (mm(ct[...], dh) * sgrad[...]).astype(BF)
@@ -273,7 +277,8 @@
     give = pl.ds(pl.multiple_of((1 - c) * 64, 64), 64)
     core_src[...] = acc[:, give, :].astype(BF)
     to_core = go([copy(core_src, core_dst, s_core, 0, other)])
-    nm[...] = (mesh.astype(F32) + normed * gain).astype(BF)
+    for h, v in zip(halves, normed):
+        nm[h, :] = (mesh[h].astype(F32) + v * gain).astype(BF)
     stored = pltpu.make_async_copy(nm, new_hbm, s_out)
     stored.start()
 

time: 66 us -> 65.6 us (level)
  no operation moved by 1% of the time
where the time goes in v3:
time: 65.6 us; the launch traced here: 65.4 us
  Pallas kernels  61.8 us (94%)
  local copies, waits for them, and re-layouts  2.93 us (4%)
    pallas_call x1, Pallas kernels, body(): pl.pallas_call(kernel, out_shape=(jax.ShapeDtypeStruct((256, 512), BF), j...  61.8 us
    unnamed x7, local copies, waits for them, and re-layouts  2.93 us

profile of v3, /device:TPU:1, one launch (start us, length us, event | category | flops | bytes accessed | tf_op | source)
XLA Modules:
  0.0 65.4 jit_solution(8416437990576325948)
XLA Ops:
  0.6 61.8 %encoder_step.1 = (bf16[256,512]{1,0:T(8,128)(2,1)}, f32[1,512]{1,0:T(1,128)}, f32[1,512]{1,0:T(1,128)}) custom-call(bf16[1024,512]{1,0:T(8,128)(2,1)} %grid_hbm.1, bf16[128,512]{1,0:T(8,128)(2,1)} %edge_hbm.1, s32[1,128]{1,0:T(1,128)} %bitcast.5, s32[1,128]{1,0:T(1,128)} %bitcast.6, s32[1,128]{1,0:T(1,128)} %bitcast.7, bf16[256,512]{1,0:T(8,128)(2,1)} %mesh_hbm.1, ...), custom_call_target="tpu_custom_call" | custom-call | tf_op jit(solution)/shard_map/encoder_step/pallas_call | solution.py:316
  62.4 0.0 copy-start.1
  62.5 1.7 %copy.18 = bf16[256,512]{1,0:T(8,128)(2,1)} copy(bf16[256,512]{1,0:T(8,128)(2,1)} %get-tuple-element.6) | data formatting | bytes 524288
  64.1 0.0 copy-done.1
  64.1 0.0 copy-start
  64.1 0.6 copy.19
  64.7 0.1 copy-done
  64.8 0.6 copy.20
Async XLA Ops:
  62.4 1.7 %copy-start.1 = (f32[1,512]{1,0:T(1,128)S(1)}, f32[1,512]{1,0:T(1,128)}, u32[]{:S(2)}) copy-start(f32[1,512]{1,0:T(1,128)} %get-tuple-element.7) | copy-start | bytes 6148
  64.1 0.7 %copy-start = (f32[1,512]{1,0:T(1,128)S(1)}, f32[1,512]{1,0:T(1,128)}, u32[]{:S(2)}) copy-start(f32[1,512]{1,0:T(1,128)} %get-tuple-element.8) | copy-start | bytes 6148

commit v4 on v3

--- a/solution.py
+++ b/solution.py
@@ -13,6 +13,9 @@
 Z_AT = (0, 1, 15, 2, 14, 3, 13, 4, 12, 5, 11, 6, 10, 7, 9, 8)
 Z_LAST = Z_AT[:0:-1]
 GROUPS = ((0, 4), (4, 4), (8, 2), (10, 2), (12, 2), (14, 2))
+
+
+LAG = 3
 
 
 def iota(shape, axis):
@@ -212,8 +215,17 @@
         ct[begin * 64 : begin * 64 + n, :] = hit
         return mm_tn(hit, hid[begin * 64 : begin * 64 + n, :])
 
+    def whole_group(k):
+        begin, count = GROUPS[k]
+        got(forward[k])
+        edge_rows(1, 3, begin, count)
+        if k < len(GROUPS) - 1:
+            turn_rows(begin, count)
+        return collect(begin, count)
+
     forward = []
-    for begin, count in GROUPS:
+    agg_h = jnp.zeros((256, 512), F32)
+    for k, (begin, count) in enumerate(GROUPS):
         new = [p for p in range(begin, begin + count) if p]
         got([s2[p] for p in new])
         got([s2_r[p] for p in new])
@@ -242,14 +254,11 @@
             gain = gain_ref[...]
             up = cot_ref[...].astype(F32) * gain
             up = up - jnp.mean(up, axis=1, keepdims=True)
-
-    agg_h = jnp.zeros((256, 512), F32)
-    for (begin, count), sent in zip(GROUPS, forward):
-        got(sent)
-        edge_rows(1, 3, begin, count)
-        agg_h += collect(begin, count)
-        if begin < GROUPS[-1][0]:
-            turn_rows(begin, count)
+        if k >= LAG:
+            agg_h += whole_group(k - LAG)
+
+    for k in range(len(GROUPS) - LAG, len(GROUPS)):
+        agg_h += whole_group(k)
 
     agg_h = agg_h.astype(BF)
     halves = (slice(0, 128), slice(128, 256))

time: 65.6 us -> 66.1 us (level)
  no operation moved by 1% of the time
where the time goes in v4:
time: 66.1 us; the launch traced here: 65.9 us
  Pallas kernels  62.4 us (94%)
  local copies, waits for them, and re-layouts  2.93 us (4%)
    pallas_call x1, Pallas kernels, body(): pl.pallas_call(kernel, out_shape=(jax.ShapeDtypeStruct((256, 512), BF), j...  62.4 us
    unnamed x7, local copies, waits for them, and re-layouts  2.93 us

profile of v4, /device:TPU:1, one launch (start us, length us, event | category | flops | bytes accessed | tf_op | source)
XLA Modules:
  0.0 65.9 jit_solution(7796980537982806356)
XLA Ops:
  0.6 62.4 %encoder_step.1 = (bf16[256,512]{1,0:T(8,128)(2,1)}, f32[1,512]{1,0:T(1,128)}, f32[1,512]{1,0:T(1,128)}) custom-call(bf16[1024,512]{1,0:T(8,128)(2,1)} %grid_hbm.1, bf16[128,512]{1,0:T(8,128)(2,1)} %edge_hbm.1, s32[1,128]{1,0:T(1,128)} %bitcast.5, s32[1,128]{1,0:T(1,128)} %bitcast.6, s32[1,128]{1,0:T(1,128)} %bitcast.7, bf16[256,512]{1,0:T(8,128)(2,1)} %mesh_hbm.1, ...), custom_call_target="tpu_custom_call" | custom-call | tf_op jit(solution)/shard_map/encoder_step/pallas_call | solution.py:325
  63.0 0.0 copy-start.1
  63.0 1.7 %copy.18 = bf16[256,512]{1,0:T(8,128)(2,1)} copy(bf16[256,512]{1,0:T(8,128)(2,1)} %get-tuple-element.6) | data formatting | bytes 524288
  64.7 0.0 copy-done.1
  64.7 0.0 copy-start
  64.7 0.6 copy.19
  65.3 0.1 copy-done
  65.4 0.6 copy.20
Async XLA Ops:
  63.0 1.7 %copy-start.1 = (f32[1,512]{1,0:T(1,128)S(1)}, f32[1,512]{1,0:T(1,128)}, u32[]{:S(2)}) copy-start(f32[1,512]{1,0:T(1,128)} %get-tuple-element.7) | copy-start | bytes 6148
  64.7 0.7 %copy-start = (f32[1,512]{1,0:T(1,128)S(1)}, f32[1,512]{1,0:T(1,128)}, u32[]{:S(2)}) copy-start(f32[1,512]{1,0:T(1,128)} %get-tuple-element.8) | copy-start | bytes 6148
